TPU v7x, 128 devices: a whole 4x4x4 slice. The times are simulated.
128 devices in a mesh: dom: 4 (over x), col: 32 (over z, y, core).
Axes of the slice: x: 4, y: 4, z: 4, core: 2. Of those that a mesh axis runs over, the one named last changes fastest.
Arguments:
- ensemble: float32 [128, 5, 96, 4096], P('dom', None, None, 'col'), may hold values from -6 to 6
- depth_class: int32 [96, 4096], P(None, 'col'), may hold values from 0 to 7
- obs_index: int32 [24576], P('col'), may hold values from 0 to 12287
- obs_value: float32 [24576], P('col'), may hold values from -4 to 16
- annealing_exponents: float32 [96, 4096], P(None, 'col'), may hold values from 0.05 to 1
Outputs:
- posterior: float32 [5, 96, 4096], P(None, None, 'col')
Inputs may be any that keep to these rules, and one draw needn't show every extreme that they name: `obs_index`: each entry is a cell of its own block of 128 columns, numbered row * 128 + column within the block; entries may repeat.
All inputs are finite; a program needn't handle non-finite values.
Results may differ from a plain program's by a relative error of at most 0.0003.
Values sent between devices are 32-bit elements; how exact they have to be, the bound alone decides.
A program may use at most 128 MiB of HBM per device.

v0:
```python
import functools

import jax
import jax.numpy as jnp
from jax import lax
from jax.experimental import pallas as pl
from jax.experimental.pallas import tpu as pltpu
from jax.sharding import PartitionSpec as P

MESH = pl.DeviceIdType.MESH
F32 = jnp.float32
BF16 = jnp.bfloat16

TIME_STEP = 0.25
CORIOLIS = 0.2
HALF_DT = 0.5 * TIME_STEP
DT_F = TIME_STEP * CORIOLIS

ROW_REACH = 8
LANES = 128
PAD = 8
FOLD = 8
SPAN = 16
CHUNK = 32


def east(q):
    return pltpu.roll(q, LANES - 1, q.ndim - 1)


def west(q):
    return pltpu.roll(q, 1, q.ndim - 1)


def shifted(q, amount):
    return pltpu.roll(q, amount % LANES, q.ndim - 1)


def pieces(q):
    first = q.astype(BF16)
    rest = q - first.astype(F32)
    second = rest.astype(BF16)
    third = (rest - second.astype(F32)).astype(BF16)
    return first, second, third


def lane_of(shape):
    return lax.broadcasted_iota(jnp.int32, shape, len(shape) - 1)


def row_of(shape):
    return lax.broadcasted_iota(jnp.int32, shape, len(shape) - 2)


def dot(a, b):
    return jnp.dot(a, b, preferred_element_type=F32)


def kernel(
    n_dom,
    n_col,
    ens_ref,
    class_ref,
    where_ref,
    value_ref,
    anneal_ref,
    out_ref,
    X,
    Y,
    DV,
    HP,
    D,
    Q,
    FE,
    SL,
    SR,
    RL,
    RR,
    OBS,
    SM,
    PART,
    TOL,
    TOR,
    HL,
    HR,
    LW,
    GIVE,
    TAKE,
    RT,
    WOWN,
    WHALO,
    load_sem,
    edge_send,
    edge_recv,
    depth_send,
    depth_recv,
    halo_send,
    halo_recv,
    part_send,
    part_recv,
    out_send,
    out_recv,
):
    members, fields, rows, _ = ens_ref.shape
    groups = members // FOLD
    pairs = members // 2
    share = rows // n_dom
    radius = LANES // 2
    me_dom = lax.axis_index("dom")
    me_col = lax.axis_index("col")
    right = lax.rem(me_col + 1, n_col)
    left = lax.rem(me_col + n_col - 1, n_col)

    def load(g):
        return pltpu.make_async_copy(
            ens_ref.at[pl.ds(g * FOLD, FOLD)],
            X.at[pl.ds(g * FOLD, FOLD), :, pl.ds(PAD, rows), :],
            load_sem.at[g],
        )

    for g in range(groups):
        load(g).start()

    barrier = pltpu.get_barrier_semaphore()
    for other in (left, right):
        pl.semaphore_signal(barrier, inc=1, device_id=(me_dom, other), device_id_type=MESH)
    for off in range(1, n_dom):
        pl.semaphore_signal(
            barrier,
            inc=1,
            device_id=(lax.rem(me_dom + off, n_dom), me_col),
            device_id_type=MESH,
        )

    zero = jnp.zeros((PAD, LANES), F32)

    def clear(m, carry):
        for f in (0, 3, 4):
            X[m, f, 0:PAD, :] = zero
            X[m, f, PAD + rows : PAD + rows + PAD, :] = zero
        return carry

    lax.fori_loop(0, members + 2 * groups, clear, 0)
    for f in (0, 3, 4):
        Y[f, 0:PAD, :] = zero
        Y[f, PAD + rows : PAD + rows + PAD, :] = zero
    DV[0:PAD, :] = zero
    DV[PAD + rows : PAD + rows + PAD, :] = zero

    plane = (rows, LANES)
    lane = lane_of(plane)
    slot = lane % SPAN
    holder = lane // SPAN
    depth = 0.5 + 0.25 * class_ref[...].astype(F32)
    D[0] = depth
    packed_depth = shifted(depth, 8)
    for i in range(1, FOLD):
        packed_depth = jnp.where(holder == i, shifted(depth, 8 + SPAN * i), packed_depth)
    SR[fields] = shifted(packed_depth, -4)
    SL[fields] = shifted(packed_depth, -8)

    pl.semaphore_wait(barrier, 2 + n_dom - 1)

    def send(source, target, there, send_sem, recv_sem):
        return pltpu.make_async_remote_copy(
            src_ref=source,
            dst_ref=target,
            send_sem=send_sem,
            recv_sem=recv_sem,
            device_id=(me_dom, there),
            device_id_type=MESH,
        )

    depth_left = send(SL.at[fields], RR.at[fields], left, depth_send.at[0], depth_recv.at[0])
    depth_right = send(SR.at[fields], RL.at[fields], right, depth_send.at[1], depth_recv.at[1])
    depth_left.start()
    depth_right.start()

    tall = (rows, 3 * rows)
    RT[...] = jnp.maximum(
        0, ROW_REACH + 1 - jnp.abs(row_of(tall) - lane_of(tall) % rows)
    ).astype(F32).astype(BF16)
    wide = (2 * LANES, 2 * LANES)
    to = lane_of(wide)
    have = row_of(wide)
    near = jnp.maximum(0, radius + 1 - jnp.abs(have % LANES - to % LANES))
    WOWN[...] = jnp.where(have // LANES == to // LANES, near, 0).astype(F32).astype(BF16)
    column = have % radius + jnp.where(have < LANES, LANES, -radius)
    near = jnp.maximum(0, radius + 1 - jnp.abs(column - to % LANES))
    WHALO[...] = (
        jnp.where((have % LANES) // radius == to // LANES, near, 0).astype(F32).astype(BF16)
    )

    where = where_ref[...]
    value = value_ref[...]
    count_obs = where.shape[1]
    in_row = row_of((rows, count_obs)) == where // LANES
    in_col = row_of((LANES, count_obs)) == where % LANES
    cols_hot = jnp.where(in_col, 1.0, 0.0).astype(BF16)

    def on_grid(piece):
        left_side = jnp.where(in_row, piece, 0.0).astype(BF16)
        return lax.dot_general(
            left_side, cols_hot, (((1,), (1,)), ((), ())), preferred_element_type=F32
        )

    def on_grid_exact(values):
        a, b, c = pieces(values)
        return on_grid(a.astype(F32)) + (on_grid(b.astype(F32)) + on_grid(c.astype(F32)))

    count = on_grid(jnp.ones_like(value))
    total_obs = on_grid_exact(value)
    squares = on_grid_exact(value * value)
    mean_obs = total_obs / jnp.maximum(count, 1.0)
    OBS[0] = -0.5 * count
    OBS[1] = mean_obs
    OBS[2] = -0.5 * (squares - total_obs * mean_obs)

    for g in range(groups):
        load(g).wait()

        def pack(f, carry, g=g):
            q = shifted(X[g * FOLD, f, pl.ds(PAD, rows), :], 8)
            for i in range(1, FOLD):
                q = jnp.where(
                    holder == i,
                    shifted(X[g * FOLD + i, f, pl.ds(PAD, rows), :], 8 + SPAN * i),
                    q,
                )
            Q[g, f] = q
            return carry

        lax.fori_loop(0, fields, pack, 0)

    def edges(f, carry):
        to_right = shifted(Q[0, f], -4)
        to_left = shifted(Q[0, f], -8)
        for g in range(1, groups):
            mine = slot // 4 == g
            to_right = jnp.where(mine, shifted(Q[g, f], 4 * g - 4), to_right)
            to_left = jnp.where(mine, shifted(Q[g, f], 4 * g - 8), to_left)
        SR[f] = to_right
        SL[f] = to_left
        return carry

    lax.fori_loop(0, fields, edges, 0)
    body = pl.ds(0, fields)
    edge_left = send(SL.at[body], RR.at[body], left, edge_send.at[0], edge_recv.at[0])
    edge_right = send(SR.at[body], RL.at[body], right, edge_send.at[1], edge_recv.at[1])
    edge_left.start()
    edge_right.start()

    def one_step(read, write, d):
        for r in range(0, rows, CHUNK):
            h = read(0, r)
            u = read(1, r)
            v = read(2, r)
            u1 = u - HALF_DT * (east(h) - west(h)) + DT_F * v
            v1 = v - HALF_DT * (read(0, r + 1) - read(0, r - 1)) - DT_F * u
            write(1, r, u1)
            write(2, r, v1)
            deep = D[d, r : r + CHUNK, :]
            du = deep * u1
            DV[PAD + r : PAD + r + CHUNK, :] = deep * v1
            HP[r : r + CHUNK, :] = h - HALF_DT * (east(du) - west(du))
            u2 = HALF_DT * u1
            v2 = HALF_DT * v1
            for f in (3, 4):
                a = read(f, r)
                write(
                    f,
                    r,
                    a - (u2 * (east(a) - west(a)) + v2 * (read(f, r + 1) - read(f, r - 1))),
                )
        for r in range(0, rows, CHUNK):
            up = DV[PAD + r + 1 : PAD + r + 1 + CHUNK, :]
            down = DV[PAD + r - 1 : PAD + r - 1 + CHUNK, :]
            write(0, r, HP[r : r + CHUNK, :] - HALF_DT * (up - down))

    def ahead(m, d):
        def read_x(f, r):
            return X[m, f, PAD + r : PAD + r + CHUNK, :]

        def write_x(f, r, q):
            X[m, f, PAD + r : PAD + r + CHUNK, :] = q

        def read_y(f, r):
            return Y[f, PAD + r : PAD + r + CHUNK, :]

        def write_y(f, r, q):
            Y[f, PAD + r : PAD + r + CHUNK, :] = q

        one_step(read_x, write_y, d)
        one_step(read_y, write_x, d)

    def ahead_main(m, carry):
        ahead(m, 0)
        return carry

    lax.fori_loop(0, members, ahead_main, 0)

    depth_left.wait()
    depth_right.wait()
    D[1] = jnp.where(slot < 8, packed_depth_of(D[0], holder), shifted(RR[fields], 8))
    D[2] = jnp.where(slot >= 8, packed_depth_of(D[0], holder), shifted(RL[fields], 4))
    edge_left.wait()
    edge_right.wait()

    def strips(f, carry):
        for g in range(groups):
            q = Q[g, f]
            X[members + g, f, pl.ds(PAD, rows), :] = jnp.where(
                slot < 8, q, shifted(RR[f], 8 - 4 * g)
            )
            X[members + groups + g, f, pl.ds(PAD, rows), :] = jnp.where(
                slot >= 8, q, shifted(RL[f], 4 - 4 * g)
            )
        return carry

    lax.fori_loop(0, fields, strips, 0)

    def ahead_strip(s, carry):
        ahead(members + s, 1 + s // groups)
        return carry

    lax.fori_loop(0, 2 * groups, ahead_strip, 0)

    def join(f, carry):
        for g in range(groups):
            FE[g, f] = jnp.where(
                slot < 8,
                X[members + g, f, pl.ds(PAD, rows), :],
                X[members + groups + g, f, pl.ds(PAD, rows), :],
            )
        return carry

    lax.fori_loop(0, fields, join, 0)

    at_edge = (lane < 4) | (lane >= LANES - 4)

    def place(i):
        return lax.rem(LANES + LANES - 8 - SPAN * i, LANES)

    def halo_left(p):
        return send(TOL.at[p], HR.at[p], left, halo_send.at[0, p], halo_recv.at[0, p])

    def halo_right(p):
        return send(TOR.at[p], HL.at[p], right, halo_send.at[1, p], halo_recv.at[1, p])

    def likelihood(p, carry):
        both = []
        for k in range(2):
            m = 2 * p + k
            edge = pltpu.roll(FE[m // FOLD, 0], place(lax.rem(m, FOLD)), 1)
            h = jnp.where(at_edge, edge, X[m, 0, pl.ds(PAD, rows), :])
            miss = OBS[1] - h
            both.append(OBS[0] * (miss * miss) + OBS[2])
        a, b, c = pieces(jnp.concatenate(both, axis=1))
        smooth = dot(RT[...], jnp.concatenate([a, b, c], axis=0))
        SM[p] = smooth
        first, second = smooth[:, :LANES], smooth[:, LANES:]
        low = lane < radius
        TOL[p] = jnp.where(low, first, shifted(second, radius))
        TOR[p] = jnp.where(low, shifted(first, radius), second)
        halo_left(p).start()
        halo_right(p).start()
        return carry

    lax.fori_loop(0, pairs, likelihood, 0)

    def columns(q, table):
        a, b, c = pieces(q)
        return dot(a, table) + (dot(b, table) + dot(c, table))

    def own_columns(p, carry):
        PART[p] = columns(SM[p], WOWN[...])
        return carry

    lax.fori_loop(0, pairs, own_columns, 0)

    def halo_wait(p, carry):
        halo_left(p).wait()
        halo_right(p).wait()
        return carry

    lax.fori_loop(0, pairs, halo_wait, 0)

    scale = 1.0 / ((ROW_REACH + 1.0) * (radius + 1.0))
    cut = (share, LANES)
    cut_lane = lane_of(cut)
    cut_edge = (cut_lane < 4) | (cut_lane >= LANES - 4)
    cut_holder = (cut_lane) // SPAN

    def weigh(b, slot_out):
        start = pl.multiple_of(b * share, 8)
        here = pl.ds(start, share)
        there = pl.ds(PAD + start, share)
        halo = jnp.concatenate([HR[:, here, :], HL[:, here, :]], axis=2)
        smooth = PART[:, here, :].reshape(pairs * share, 2 * LANES) + columns(
            halo.reshape(pairs * share, 2 * LANES), WHALO[...]
        )
        smooth = smooth.reshape(pairs, share, 2 * LANES)
        power = anneal_ref[here, :] * scale
        peak = None
        for p in range(pairs):
            for k in range(2):
                logw = power * smooth[p, :, k * LANES : (k + 1) * LANES]
                LW[2 * p + k] = logw
                peak = logw if peak is None else jnp.maximum(peak, logw)
        total = jnp.zeros(cut, F32)
        sums = [jnp.zeros(cut, F32) for _ in range(fields)]
        edge_sums = [jnp.zeros(cut, F32) for _ in range(fields)]
        for g in range(groups):
            packed = None
            for i in range(FOLD):
                m = g * FOLD + i
                w = jnp.exp(LW[m] - peak)
                total = total + w
                for f in range(fields):
                    sums[f] = sums[f] + w * X[m, f, there, :]
                moved = shifted(w, 8 + SPAN * i)
                packed = moved if packed is None else jnp.where(cut_holder == i, moved, packed)
            for f in range(fields):
                edge_sums[f] = edge_sums[f] + packed * FE[g, f, here, :]
        GIVE[slot_out, 0] = peak
        GIVE[slot_out, 1] = total
        for f in range(fields):
            e = edge_sums[f]
            e = e + shifted(e, SPAN)
            e = e + shifted(e, 2 * SPAN)
            e = e + shifted(e, 4 * SPAN)
            GIVE[slot_out, 2 + f] = jnp.where(cut_edge, shifted(e, LANES - 8), sums[f])

    def give(off):
        return pltpu.make_async_remote_copy(
            src_ref=GIVE.at[off],
            dst_ref=TAKE.at[off - 1],
            send_sem=part_send.at[off - 1],
            recv_sem=part_recv.at[off - 1],
            device_id=(lax.rem(me_dom + off, n_dom), me_col),
            device_id_type=MESH,
        )

    def offset(j):
        return 2 + j - 3 * (j // 2)

    def weigh_others(j, carry):
        off = offset(j)
        weigh(lax.rem(me_dom + off, n_dom), off)
        give(off).start()
        return carry

    lax.fori_loop(0, n_dom - 1, weigh_others, 0)
    weigh(me_dom, 0)
    for off in range(1, n_dom):
        give(off).wait()

    peaks = [GIVE[0, 0]] + [TAKE[k, 0] for k in range(n_dom - 1)]
    peak = functools.reduce(jnp.maximum, peaks)
    factors = [jnp.exp(q - peak) for q in peaks]

    def joined(f):
        result = factors[0] * GIVE[0, f]
        for k in range(n_dom - 1):
            result = result + factors[k + 1] * TAKE[k, f]
        return result

    total = joined(1)
    here = pl.ds(pl.multiple_of(me_dom * share, 8), share)
    for f in range(fields):
        out_ref[f, here, :] = joined(2 + f) / total

    def hand_out(off):
        return pltpu.make_async_remote_copy(
            src_ref=out_ref.at[:, here, :],
            dst_ref=out_ref.at[:, here, :],
            send_sem=out_send.at[off - 1],
            recv_sem=out_recv.at[off - 1],
            device_id=(lax.rem(me_dom + off, n_dom), me_col),
            device_id_type=MESH,
        )

    for off in range(1, n_dom):
        hand_out(off).start()
    for off in range(1, n_dom):
        hand_out(off).wait()


def packed_depth_of(depth, holder):
    packed = shifted(depth, 8)
    for i in range(1, FOLD):
        packed = jnp.where(holder == i, shifted(depth, 8 + SPAN * i), packed)
    return packed


def solution(mesh):
    n_dom = mesh.shape["dom"]
    n_col = mesh.shape["col"]

    def on_device(ensemble, depth_class, obs_index, obs_value, annealing_exponents):
        members, fields, rows, lanes = ensemble.shape
        groups = members // FOLD
        pairs = members // 2
        share = rows // n_dom
        tall = rows + 2 * PAD
        vm = pl.BlockSpec(memory_space=pltpu.VMEM)
        dma = pltpu.SemaphoreType.DMA
        return pl.pallas_call(
            functools.partial(kernel, n_dom, n_col),
            out_shape=jax.ShapeDtypeStruct((fields, rows, lanes), F32),
            in_specs=[pl.BlockSpec(memory_space=pl.ANY), vm, vm, vm, vm],
            out_specs=vm,
            scratch_shapes=[
                pltpu.VMEM((members + 2 * groups, fields, tall, lanes), F32),
                pltpu.VMEM((fields, tall, lanes), F32),
                pltpu.VMEM((tall, lanes), F32),
                pltpu.VMEM((rows, lanes), F32),
                pltpu.VMEM((3, rows, lanes), F32),
                pltpu.VMEM((groups, fields, rows, lanes), F32),
                pltpu.VMEM((groups, fields, rows, lanes), F32),
                pltpu.VMEM((fields + 1, rows, lanes), F32),
                pltpu.VMEM((fields + 1, rows, lanes), F32),
                pltpu.VMEM((fields + 1, rows, lanes), F32),
                pltpu.VMEM((fields + 1, rows, lanes), F32),
                pltpu.VMEM((3, rows, lanes), F32),
                pltpu.VMEM((pairs, rows, 2 * lanes), F32),
                pltpu.VMEM((pairs, rows, 2 * lanes), F32),
                pltpu.VMEM((pairs, rows, lanes), F32),
                pltpu.VMEM((pairs, rows, lanes), F32),
                pltpu.VMEM((pairs, rows, lanes), F32),
                pltpu.VMEM((pairs, rows, lanes), F32),
                pltpu.VMEM((members, share, lanes), F32),
                pltpu.VMEM((n_dom, fields + 2, share, lanes), F32),
                pltpu.VMEM((n_dom - 1, fields + 2, share, lanes), F32),
                pltpu.VMEM((rows, 3 * rows), BF16),
                pltpu.VMEM((2 * lanes, 2 * lanes), BF16),
                pltpu.VMEM((2 * lanes, 2 * lanes), BF16),
                dma((groups,)),
                dma((2,)),
                dma((2,)),
                dma((2,)),
                dma((2,)),
                dma((2, pairs)),
                dma((2, pairs)),
                dma((n_dom - 1,)),
                dma((n_dom - 1,)),
                dma((n_dom - 1,)),
                dma((n_dom - 1,)),
            ],
            compiler_params=pltpu.CompilerParams(
                collective_id=0, has_side_effects=True, vmem_limit_bytes=48 * 1024 * 1024
            ),
            cost_estimate=pl.CostEstimate(
                flops=200_000_000, bytes_accessed=9_000_000, transcendentals=400_000
            ),
        )(
            ensemble,
            depth_class,
            obs_index.reshape(1, -1),
            obs_value.reshape(1, -1),
            annealing_exponents,
        )

    in_specs = (P("dom", None, None, "col"), P(None, "col"), P("col"), P("col"), P(None, "col"))
    out_specs = P(None, None, "col")
    return jax.shard_map(
        on_device, mesh=mesh, in_specs=in_specs, out_specs=out_specs, check_vma=False
    )
```

profile of v0, /device:TPU:0, one launch (start us, length us, event | category | flops | bytes accessed | tf_op | source)
XLA Modules:
  0.0 56.2 jit_solution(7936496742670293690)
XLA Ops:
  0.0 0.7 %reshape.6.where_ref = s32[1,768]{1,0:T(1,128)S(1)} reshape(s32[768]{0:T(1024)} %param.7) | data formatting | bytes 6144 | tf_op jit(solution)/shard_map/reshape | solution.py:559
  0.7 0.7 %reshape.7.value_ref = f32[1,768]{1,0:T(1,128)S(1)} reshape(f32[768]{0:T(1024)} %param.8) | data formatting | bytes 6144 | tf_op jit(solution)/shard_map/reshape | solution.py:560
  1.4 0.0 copy-start
  1.4 0.8 %copy-done = s32[96,128]{1,0:T(8,128)S(1)} copy-done((s32[96,128]{1,0:T(8,128)S(1)}, s32[96,128]{1,0:T(8,128)}, u32[]{:S(2)}) %copy-start) | copy-done | bytes 49176
  2.2 0.0 copy-start.1
  2.2 0.8 %copy-done.1 = f32[96,128]{1,0:T(8,128)S(1)} copy-done((f32[96,128]{1,0:T(8,128)S(1)}, f32[96,128]{1,0:T(8,128)}, u32[]{:S(2)}) %copy-start.1) | copy-done | bytes 49176
  3.0 52.5 %shard_map.55 = f32[5,96,128]{2,1,0:T(8,128)S(1)} custom-call(f32[32,5,96,128]{3,2,1,0:T(8,128)} %ens_ref.1, s32[96,128]{1,0:T(8,128)S(1)} %copy-done, s32[1,768]{1,0:T(1,128)S(1)} %reshape.6.where_ref, f32[1,768]{1,0:T(1,128)S(1)} %reshape.7.value_ref, f32[96,128]{1,0:T(8,128)S(1)} %copy-done.1), custom_call_target="tpu_custom_call" | custom-call | flops 200000000 | bytes 9000000 | tf_op jit(solution)/shard_map/pallas_call | solution.py:508
  55.5 0.7 %copy.7 = f32[5,96,128]{2,1,0:T(8,128)} copy(f32[5,96,128]{2,1,0:T(8,128)S(1)} %shard_map.55) | data formatting | bytes 491520
Async XLA Ops:
  1.4 0.8 %copy-start = (s32[96,128]{1,0:T(8,128)S(1)}, s32[96,128]{1,0:T(8,128)}, u32[]{:S(2)}) copy-start(s32[96,128]{1,0:T(8,128)} %class_ref.1) | copy-start | bytes 147460
  2.2 0.8 %copy-start.1 = (f32[96,128]{1,0:T(8,128)S(1)}, f32[96,128]{1,0:T(8,128)}, u32[]{:S(2)}) copy-start(f32[96,128]{1,0:T(8,128)} %anneal_ref.1) | copy-start | bytes 147460
where the time goes:
time: 56.5 us; the launch traced here: 56.2 us
  Pallas kernels  52.5 us (93%)
  local copies, waits for them, and re-layouts  3.67 us (6%)
    pallas_call x1, Pallas kernels, on_device(): pl.pallas_call(functools.partial(kernel, n_dom, n_col), out_shape=jax.Sha...  52.5 us
    unnamed x5, local copies, waits for them, and re-layouts  2.29 us

commit v1 on v0

--- a/solution.py
+++ b/solution.py
@@ -22,6 +22,7 @@
 FOLD = 8
 SPAN = 16
 CHUNK = 32
+EARLY = 16
 
 
 def east(q):
@@ -66,10 +67,17 @@
     anneal_ref,
     out_ref,
     X,
+    U1,
     Y,
+    YT,
     DV,
     HP,
+    CLS,
+    WHERE,
+    VALUE,
+    ANNEAL,
     D,
+    QD,
     Q,
     FE,
     SL,
@@ -89,11 +97,11 @@
     RT,
     WOWN,
     WHALO,
+    DX,
+    small_sem,
     load_sem,
     edge_send,
     edge_recv,
-    depth_send,
-    depth_recv,
     halo_send,
     halo_recv,
     part_send,
@@ -106,20 +114,34 @@
     pairs = members // 2
     share = rows // n_dom
     radius = LANES // 2
+    flow = 3
     me_dom = lax.axis_index("dom")
     me_col = lax.axis_index("col")
     right = lax.rem(me_col + 1, n_col)
     left = lax.rem(me_col + n_col - 1, n_col)
-
-    def load(g):
+    inner = pl.ds(PAD, rows)
+
+    def load(g, tracers):
+        which = pl.ds(flow, fields - flow) if tracers else pl.ds(0, flow)
         return pltpu.make_async_copy(
-            ens_ref.at[pl.ds(g * FOLD, FOLD)],
-            X.at[pl.ds(g * FOLD, FOLD), :, pl.ds(PAD, rows), :],
-            load_sem.at[g],
-        )
-
+            ens_ref.at[pl.ds(g * FOLD, FOLD), which],
+            X.at[pl.ds(g * FOLD, FOLD), which, inner, :],
+            load_sem.at[int(tracers), g],
+        )
+
+    small = [
+        pltpu.make_async_copy(source, target, small_sem.at[k])
+        for k, (source, target) in enumerate(
+            ((class_ref, CLS), (where_ref, WHERE), (value_ref, VALUE), (anneal_ref, ANNEAL))
+        )
+    ]
+    load(0, False).start()
+    for copy in small:
+        copy.start()
+    for g in range(1, groups):
+        load(g, False).start()
     for g in range(groups):
-        load(g).start()
+        load(g, True).start()
 
     barrier = pltpu.get_barrier_semaphore()
     for other in (left, right):
@@ -141,40 +163,9 @@
         return carry
 
     lax.fori_loop(0, members + 2 * groups, clear, 0)
-    for f in (0, 3, 4):
-        Y[f, 0:PAD, :] = zero
-        Y[f, PAD + rows : PAD + rows + PAD, :] = zero
-    DV[0:PAD, :] = zero
-    DV[PAD + rows : PAD + rows + PAD, :] = zero
-
-    plane = (rows, LANES)
-    lane = lane_of(plane)
-    slot = lane % SPAN
-    holder = lane // SPAN
-    depth = 0.5 + 0.25 * class_ref[...].astype(F32)
-    D[0] = depth
-    packed_depth = shifted(depth, 8)
-    for i in range(1, FOLD):
-        packed_depth = jnp.where(holder == i, shifted(depth, 8 + SPAN * i), packed_depth)
-    SR[fields] = shifted(packed_depth, -4)
-    SL[fields] = shifted(packed_depth, -8)
-
-    pl.semaphore_wait(barrier, 2 + n_dom - 1)
-
-    def send(source, target, there, send_sem, recv_sem):
-        return pltpu.make_async_remote_copy(
-            src_ref=source,
-            dst_ref=target,
-            send_sem=send_sem,
-            recv_sem=recv_sem,
-            device_id=(me_dom, there),
-            device_id_type=MESH,
-        )
-
-    depth_left = send(SL.at[fields], RR.at[fields], left, depth_send.at[0], depth_recv.at[0])
-    depth_right = send(SR.at[fields], RL.at[fields], right, depth_send.at[1], depth_recv.at[1])
-    depth_left.start()
-    depth_right.start()
+    for padded in (Y.at[0], YT.at[0], YT.at[1], DV):
+        padded[0:PAD, :] = zero
+        padded[PAD + rows : PAD + rows + PAD, :] = zero
 
     tall = (rows, 3 * rows)
     RT[...] = jnp.maximum(
@@ -191,46 +182,39 @@
         jnp.where((have % LANES) // radius == to // LANES, near, 0).astype(F32).astype(BF16)
     )
 
-    where = where_ref[...]
-    value = value_ref[...]
-    count_obs = where.shape[1]
-    in_row = row_of((rows, count_obs)) == where // LANES
-    in_col = row_of((LANES, count_obs)) == where % LANES
-    cols_hot = jnp.where(in_col, 1.0, 0.0).astype(BF16)
-
-    def on_grid(piece):
-        left_side = jnp.where(in_row, piece, 0.0).astype(BF16)
-        return lax.dot_general(
-            left_side, cols_hot, (((1,), (1,)), ((), ())), preferred_element_type=F32
-        )
-
-    def on_grid_exact(values):
-        a, b, c = pieces(values)
-        return on_grid(a.astype(F32)) + (on_grid(b.astype(F32)) + on_grid(c.astype(F32)))
-
-    count = on_grid(jnp.ones_like(value))
-    total_obs = on_grid_exact(value)
-    squares = on_grid_exact(value * value)
-    mean_obs = total_obs / jnp.maximum(count, 1.0)
-    OBS[0] = -0.5 * count
-    OBS[1] = mean_obs
-    OBS[2] = -0.5 * (squares - total_obs * mean_obs)
-
-    for g in range(groups):
-        load(g).wait()
-
-        def pack(f, carry, g=g):
-            q = shifted(X[g * FOLD, f, pl.ds(PAD, rows), :], 8)
+    wide = (2 * LANES, LANES)
+    ahead_by = (row_of(wide) - lane_of(wide)) % LANES
+    DX[...] = (
+        jnp.where(ahead_by == 1, HALF_DT, jnp.where(ahead_by == LANES - 1, -HALF_DT, 0.0))
+    ).astype(BF16)
+
+    for copy in small:
+        copy.wait()
+
+    plane = (rows, LANES)
+    lane = lane_of(plane)
+    slot = lane % SPAN
+    holder = lane // SPAN
+    depth = 0.5 + 0.25 * CLS[...].astype(F32)
+    D[0] = depth
+    packed_depth = shifted(depth, 8)
+    for i in range(1, FOLD):
+        packed_depth = jnp.where(holder == i, shifted(depth, 8 + SPAN * i), packed_depth)
+    QD[...] = packed_depth
+    SR[0] = shifted(packed_depth, -4)
+    SL[0] = shifted(packed_depth, -8)
+
+    def pack_group(g, first, last):
+        def pack(f, carry):
+            q = shifted(X[g * FOLD, f, inner, :], 8)
             for i in range(1, FOLD):
                 q = jnp.where(
-                    holder == i,
-                    shifted(X[g * FOLD + i, f, pl.ds(PAD, rows), :], 8 + SPAN * i),
-                    q,
+                    holder == i, shifted(X[g * FOLD + i, f, inner, :], 8 + SPAN * i), q
                 )
             Q[g, f] = q
             return carry
 
-        lax.fori_loop(0, fields, pack, 0)
+        lax.fori_loop(first, last, pack, 0)
 
     def edges(f, carry):
         to_right = shifted(Q[0, f], -4)
@@ -239,102 +223,184 @@
             mine = slot // 4 == g
             to_right = jnp.where(mine, shifted(Q[g, f], 4 * g - 4), to_right)
             to_left = jnp.where(mine, shifted(Q[g, f], 4 * g - 8), to_left)
-        SR[f] = to_right
-        SL[f] = to_left
-        return carry
-
-    lax.fori_loop(0, fields, edges, 0)
-    body = pl.ds(0, fields)
-    edge_left = send(SL.at[body], RR.at[body], left, edge_send.at[0], edge_recv.at[0])
-    edge_right = send(SR.at[body], RL.at[body], right, edge_send.at[1], edge_recv.at[1])
-    edge_left.start()
-    edge_right.start()
-
-    def one_step(read, write, d):
+        SR[1 + f] = to_right
+        SL[1 + f] = to_left
+        return carry
+
+    def send(source, target, there, send_sem, recv_sem):
+        return pltpu.make_async_remote_copy(
+            src_ref=source,
+            dst_ref=target,
+            send_sem=send_sem,
+            recv_sem=recv_sem,
+            device_id=(me_dom, there),
+            device_id_type=MESH,
+        )
+
+    def edge_copies(tracers):
+        which = pl.ds(1 + flow, fields - flow) if tracers else pl.ds(0, 1 + flow)
+        k = int(tracers)
+        return (
+            send(SL.at[which], RR.at[which], left, edge_send.at[k, 0], edge_recv.at[k, 0]),
+            send(SR.at[which], RL.at[which], right, edge_send.at[k, 1], edge_recv.at[k, 1]),
+        )
+
+    for g in range(groups):
+        load(g, False).wait()
+        pack_group(g, 0, flow)
+    lax.fori_loop(0, flow, edges, 0)
+    pl.semaphore_wait(barrier, 2 + n_dom - 1)
+    flow_edges = edge_copies(False)
+    for copy in flow_edges:
+        copy.start()
+
+    for g in range(groups):
+        load(g, True).wait()
+        pack_group(g, flow, fields)
+    lax.fori_loop(flow, fields, edges, 0)
+    tracer_edges = edge_copies(True)
+    for copy in tracer_edges:
+        copy.start()
+
+    where = WHERE[...]
+    value = VALUE[...]
+    parts = where.shape[0]
+
+    def along(q):
+        return jnp.concatenate([q[j : j + 1, :] for j in range(parts)], axis=1)
+
+    obs_row = along(where // LANES)
+    obs_col = along(where % LANES)
+    obs_value = along(value)
+    count_obs = parts * LANES
+    in_row = row_of((rows, count_obs)) == obs_row
+    in_col = row_of((LANES, count_obs)) == obs_col
+    cols_hot = jnp.where(in_col, 1.0, 0.0).astype(BF16)
+
+    def on_grid(piece):
+        left_side = jnp.where(in_row, piece, 0.0).astype(BF16)
+        return lax.dot_general(
+            left_side, cols_hot, (((1,), (1,)), ((), ())), preferred_element_type=F32
+        )
+
+    def on_grid_exact(values):
+        a, b, c = pieces(values)
+        return on_grid(a.astype(F32)) + (on_grid(b.astype(F32)) + on_grid(c.astype(F32)))
+
+    count = on_grid(jnp.ones_like(obs_value))
+    total_obs = on_grid_exact(obs_value)
+    squares = on_grid_exact(obs_value * obs_value)
+    mean_obs = total_obs / jnp.maximum(count, 1.0)
+    OBS[0] = -0.5 * count
+    OBS[1] = mean_obs
+    OBS[2] = -0.5 * (squares - total_obs * mean_obs)
+
+    def flow_step(h_ref, u_ref, v_ref, to_h, to_u, to_v, d):
         for r in range(0, rows, CHUNK):
-            h = read(0, r)
-            u = read(1, r)
-            v = read(2, r)
+            cut = pl.ds(r, CHUNK)
+            mid = pl.ds(PAD + r, CHUNK)
+            h = h_ref[mid, :]
+            u = u_ref(r)
+            v = v_ref(r)
             u1 = u - HALF_DT * (east(h) - west(h)) + DT_F * v
-            v1 = v - HALF_DT * (read(0, r + 1) - read(0, r - 1)) - DT_F * u
-            write(1, r, u1)
-            write(2, r, v1)
-            deep = D[d, r : r + CHUNK, :]
+            slope = h_ref[pl.ds(PAD + r + 1, CHUNK), :] - h_ref[pl.ds(PAD + r - 1, CHUNK), :]
+            v1 = v - HALF_DT * slope - DT_F * u
+            to_u(r, u1)
+            to_v(r, v1)
+            deep = D[d, cut, :]
             du = deep * u1
-            DV[PAD + r : PAD + r + CHUNK, :] = deep * v1
-            HP[r : r + CHUNK, :] = h - HALF_DT * (east(du) - west(du))
-            u2 = HALF_DT * u1
-            v2 = HALF_DT * v1
-            for f in (3, 4):
-                a = read(f, r)
-                write(
-                    f,
-                    r,
-                    a - (u2 * (east(a) - west(a)) + v2 * (read(f, r + 1) - read(f, r - 1))),
-                )
+            DV[mid, :] = deep * v1
+            HP[cut, :] = h - HALF_DT * (east(du) - west(du))
         for r in range(0, rows, CHUNK):
-            up = DV[PAD + r + 1 : PAD + r + 1 + CHUNK, :]
-            down = DV[PAD + r - 1 : PAD + r - 1 + CHUNK, :]
-            write(0, r, HP[r : r + CHUNK, :] - HALF_DT * (up - down))
-
-    def ahead(m, d):
-        def read_x(f, r):
-            return X[m, f, PAD + r : PAD + r + CHUNK, :]
-
-        def write_x(f, r, q):
-            X[m, f, PAD + r : PAD + r + CHUNK, :] = q
-
-        def read_y(f, r):
-            return Y[f, PAD + r : PAD + r + CHUNK, :]
-
-        def write_y(f, r, q):
-            Y[f, PAD + r : PAD + r + CHUNK, :] = q
-
-        one_step(read_x, write_y, d)
-        one_step(read_y, write_x, d)
-
-    def ahead_main(m, carry):
-        ahead(m, 0)
-        return carry
-
-    lax.fori_loop(0, members, ahead_main, 0)
-
-    depth_left.wait()
-    depth_right.wait()
-    D[1] = jnp.where(slot < 8, packed_depth_of(D[0], holder), shifted(RR[fields], 8))
-    D[2] = jnp.where(slot >= 8, packed_depth_of(D[0], holder), shifted(RL[fields], 4))
-    edge_left.wait()
-    edge_right.wait()
+            up = DV[pl.ds(PAD + r + 1, CHUNK), :]
+            down = DV[pl.ds(PAD + r - 1, CHUNK), :]
+            to_h[pl.ds(PAD + r, CHUNK), :] = HP[pl.ds(r, CHUNK), :] - HALF_DT * (up - down)
+
+    def flow_ahead(m, d):
+        def get_x(f):
+            return lambda r: X[m, f, pl.ds(PAD + r, CHUNK), :]
+
+        def get_u(f):
+            return lambda r: U1[m, f, pl.ds(r, CHUNK), :]
+
+        def put_x(f):
+            def put(r, q):
+                X[m, f, pl.ds(PAD + r, CHUNK), :] = q
+
+            return put
+
+        def put_u(f):
+            def put(r, q):
+                U1[m, f, pl.ds(r, CHUNK), :] = q
+
+            return put
+
+        flow_step(X.at[m, 0], get_x(1), get_x(2), Y.at[0], put_u(0), put_u(1), d)
+        flow_step(Y.at[0], get_u(0), get_u(1), X.at[m, 0], put_x(1), put_x(2), d)
+
+    def tracers_ahead(m):
+        for step in range(2):
+            ends = [(X.at[m, f], YT.at[f - flow]) for f in range(flow, fields)]
+            if step == 1:
+                ends = [(target, source) for source, target in ends]
+            split = []
+            for source, _ in ends:
+                a = source[inner, :]
+                first = a.astype(BF16)
+                second = (a - first.astype(F32)).astype(BF16)
+                split.append(jnp.concatenate([first, second], axis=1))
+            across = dot(jnp.concatenate(split, axis=0), DX[...])
+            for r in range(0, rows, CHUNK):
+                mid = pl.ds(PAD + r, CHUNK)
+                if step == 0:
+                    u = U1[m, 0, pl.ds(r, CHUNK), :]
+                    v = U1[m, 1, pl.ds(r, CHUNK), :]
+                else:
+                    u = X[m, 1, mid, :]
+                    v = X[m, 2, mid, :]
+                v = HALF_DT * v
+                for k, (source, target) in enumerate(ends):
+                    slope = (
+                        source[pl.ds(PAD + r + 1, CHUNK), :] - source[pl.ds(PAD + r - 1, CHUNK), :]
+                    )
+                    steep = across[k * rows + r : k * rows + r + CHUNK, :]
+                    target[mid, :] = source[mid, :] - (u * steep + v * slope)
+
+    def flow_main(m, carry):
+        flow_ahead(m, 0)
+        return carry
+
+    early = EARLY
+    lax.fori_loop(0, early, flow_main, 0)
 
     def strips(f, carry):
         for g in range(groups):
             q = Q[g, f]
-            X[members + g, f, pl.ds(PAD, rows), :] = jnp.where(
-                slot < 8, q, shifted(RR[f], 8 - 4 * g)
+            X[members + g, f, inner, :] = jnp.where(slot < 8, q, shifted(RR[1 + f], 8 - 4 * g))
+            X[members + groups + g, f, inner, :] = jnp.where(
+                slot >= 8, q, shifted(RL[1 + f], 4 - 4 * g)
             )
-            X[members + groups + g, f, pl.ds(PAD, rows), :] = jnp.where(
-                slot >= 8, q, shifted(RL[f], 4 - 4 * g)
-            )
-        return carry
-
-    lax.fori_loop(0, fields, strips, 0)
-
-    def ahead_strip(s, carry):
-        ahead(members + s, 1 + s // groups)
-        return carry
-
-    lax.fori_loop(0, 2 * groups, ahead_strip, 0)
+        return carry
 
     def join(f, carry):
         for g in range(groups):
             FE[g, f] = jnp.where(
-                slot < 8,
-                X[members + g, f, pl.ds(PAD, rows), :],
-                X[members + groups + g, f, pl.ds(PAD, rows), :],
+                slot < 8, X[members + g, f, inner, :], X[members + groups + g, f, inner, :]
             )
         return carry
 
-    lax.fori_loop(0, fields, join, 0)
+    for copy in flow_edges:
+        copy.wait()
+    D[1] = jnp.where(slot < 8, QD[...], shifted(RR[0], 8))
+    D[2] = jnp.where(slot >= 8, QD[...], shifted(RL[0], 4))
+    lax.fori_loop(0, flow, strips, 0)
+
+    def flow_strip(s, carry):
+        flow_ahead(members + s, 1 + s // groups)
+        return carry
+
+    lax.fori_loop(0, 2 * groups, flow_strip, 0)
+    join(0, 0)
 
     at_edge = (lane < 4) | (lane >= LANES - 4)
 
@@ -352,7 +418,7 @@
         for k in range(2):
             m = 2 * p + k
             edge = pltpu.roll(FE[m // FOLD, 0], place(lax.rem(m, FOLD)), 1)
-            h = jnp.where(at_edge, edge, X[m, 0, pl.ds(PAD, rows), :])
+            h = jnp.where(at_edge, edge, X[m, 0, inner, :])
             miss = OBS[1] - h
             both.append(OBS[0] * (miss * miss) + OBS[2])
         a, b, c = pieces(jnp.concatenate(both, axis=1))
@@ -360,13 +426,31 @@
         SM[p] = smooth
         first, second = smooth[:, :LANES], smooth[:, LANES:]
         low = lane < radius
-        TOL[p] = jnp.where(low, first, shifted(second, radius))
-        TOR[p] = jnp.where(low, shifted(first, radius), second)
+        turned = shifted(jnp.where(low, second, first), radius)
+        TOL[p] = jnp.where(low, first, turned)
+        TOR[p] = jnp.where(low, turned, second)
         halo_left(p).start()
         halo_right(p).start()
         return carry
 
-    lax.fori_loop(0, pairs, likelihood, 0)
+    def flow_and_likelihood(p, carry):
+        ahead = p + early // 2
+        flow_ahead(2 * ahead, 0)
+        flow_ahead(2 * ahead + 1, 0)
+        return likelihood(p, carry)
+
+    lax.fori_loop(0, pairs - early // 2, flow_and_likelihood, 0)
+    lax.fori_loop(pairs - early // 2, pairs, likelihood, 0)
+
+    def tracers_main(m, carry):
+        tracers_ahead(m)
+        return carry
+
+    for copy in tracer_edges:
+        copy.wait()
+    lax.fori_loop(flow, fields, strips, 0)
+    lax.fori_loop(0, members + 2 * groups, tracers_main, 0, unroll=4)
+    lax.fori_loop(1, fields, join, 0)
 
     def columns(q, table):
         a, b, c = pieces(q)
@@ -376,7 +460,7 @@
         PART[p] = columns(SM[p], WOWN[...])
         return carry
 
-    lax.fori_loop(0, pairs, own_columns, 0)
+    lax.fori_loop(0, pairs, own_columns, 0, unroll=4)
 
     def halo_wait(p, carry):
         halo_left(p).wait()
@@ -400,7 +484,7 @@
             halo.reshape(pairs * share, 2 * LANES), WHALO[...]
         )
         smooth = smooth.reshape(pairs, share, 2 * LANES)
-        power = anneal_ref[here, :] * scale
+        power = ANNEAL[here, :] * scale
         peak = None
         for p in range(pairs):
             for k in range(2):
@@ -486,13 +570,6 @@
         hand_out(off).wait()
 
 
-def packed_depth_of(depth, holder):
-    packed = shifted(depth, 8)
-    for i in range(1, FOLD):
-        packed = jnp.where(holder == i, shifted(depth, 8 + SPAN * i), packed)
-    return packed
-
-
 def solution(mesh):
     n_dom = mesh.shape["dom"]
     n_col = mesh.shape["col"]
@@ -508,14 +585,21 @@
         return pl.pallas_call(
             functools.partial(kernel, n_dom, n_col),
             out_shape=jax.ShapeDtypeStruct((fields, rows, lanes), F32),
-            in_specs=[pl.BlockSpec(memory_space=pl.ANY), vm, vm, vm, vm],
+            in_specs=[pl.BlockSpec(memory_space=pl.ANY)] * 5,
             out_specs=vm,
             scratch_shapes=[
                 pltpu.VMEM((members + 2 * groups, fields, tall, lanes), F32),
-                pltpu.VMEM((fields, tall, lanes), F32),
+                pltpu.VMEM((members + 2 * groups, 2, rows, lanes), F32),
+                pltpu.VMEM((1, tall, lanes), F32),
+                pltpu.VMEM((2, tall, lanes), F32),
                 pltpu.VMEM((tall, lanes), F32),
                 pltpu.VMEM((rows, lanes), F32),
+                pltpu.VMEM((rows, lanes), jnp.int32),
+                pltpu.VMEM((obs_index.shape[0] // lanes, lanes), jnp.int32),
+                pltpu.VMEM((obs_index.shape[0] // lanes, lanes), F32),
+                pltpu.VMEM((rows, lanes), F32),
                 pltpu.VMEM((3, rows, lanes), F32),
+                pltpu.VMEM((rows, lanes), F32),
                 pltpu.VMEM((groups, fields, rows, lanes), F32),
                 pltpu.VMEM((groups, fields, rows, lanes), F32),
                 pltpu.VMEM((fields + 1, rows, lanes), F32),
@@ -535,11 +619,11 @@
                 pltpu.VMEM((rows, 3 * rows), BF16),
                 pltpu.VMEM((2 * lanes, 2 * lanes), BF16),
                 pltpu.VMEM((2 * lanes, 2 * lanes), BF16),
-                dma((groups,)),
-                dma((2,)),
-                dma((2,)),
-                dma((2,)),
-                dma((2,)),
+                pltpu.VMEM((2 * lanes, lanes), BF16),
+                dma((4,)),
+                dma((2, groups)),
+                dma((2, 2)),
+                dma((2, 2)),
                 dma((2, pairs)),
                 dma((2, pairs)),
                 dma((n_dom - 1,)),
@@ -548,7 +632,7 @@
                 dma((n_dom - 1,)),
             ],
             compiler_params=pltpu.CompilerParams(
-                collective_id=0, has_side_effects=True, vmem_limit_bytes=48 * 1024 * 1024
+                collective_id=0, has_side_effects=True, vmem_limit_bytes=62 * 1024 * 1024
             ),
             cost_estimate=pl.CostEstimate(
                 flops=200_000_000, bytes_accessed=9_000_000, transcendentals=400_000
@@ -556,8 +640,8 @@
         )(
             ensemble,
             depth_class,
-            obs_index.reshape(1, -1),
-            obs_value.reshape(1, -1),
+            obs_index.reshape(-1, lanes),
+            obs_value.reshape(-1, lanes),
             annealing_exponents,
         )
 

time: 56.5 us -> 46.6 us (0.82)
  Pallas kernels: 52.5 us -> 44.8 us
  local copies, waits for them, and re-layouts: 3.67 us -> 1.65 us
    pallas_call x1, Pallas kernels: 52.5 us -> 44.8 us  [on_device(): pl.pallas_call(functools.partial(kernel, n_dom, n_col), out_shape=jax.Sha...]
    reshape x2 -> x0, local copies, waits for them, and re-layouts: 1.38 us -> none  [the longest x1 0.69 us: on_device(): obs_index.reshape(1, -1)]
    unnamed x5 -> x1, local copies, waits for them, and re-layouts: 2.29 us -> 1.65 us
where the time goes in v1:
time: 46.6 us; the launch traced here: 46.4 us
  Pallas kernels  44.8 us (96%)
  local copies, waits for them, and re-layouts  1.65 us (4%)
    pallas_call x1, Pallas kernels, on_device(): pl.pallas_call(functools.partial(kernel, n_dom, n_col), out_shape=jax.Sha...  44.8 us
    unnamed x1, local copies, waits for them, and re-layouts  1.65 us

profile of v1, /device:TPU:0, one launch (start us, length us, event | category | flops | bytes accessed | tf_op | source)
XLA Modules:
  0.0 46.4 jit_solution(10886990612785073142)
XLA Ops:
  0.0 44.8 %shard_map.55 = f32[5,96,128]{2,1,0:T(8,128)} custom-call(f32[32,5,96,128]{3,2,1,0:T(8,128)} %ens_ref.1, s32[96,128]{1,0:T(8,128)} %class_ref.1, s32[6,128]{1,0:T(8,128)} %bitcast.2, f32[6,128]{1,0:T(8,128)} %bitcast.3, f32[96,128]{1,0:T(8,128)} %anneal_ref.1), custom_call_target="tpu_custom_call" | custom-call | flops 200000000 | bytes 9000000 | tf_op jit(solution)/shard_map/pallas_call | solution.py:585
  44.8 1.7 %copy.7 = f32[5,96,128]{2,1,0:T(8,128)} copy(f32[5,96,128]{2,1,0:T(8,128)} %shard_map.55) | data formatting | bytes 491520

commit v2 on v1

--- a/solution.py
+++ b/solution.py
@@ -22,15 +22,8 @@
 FOLD = 8
 SPAN = 16
 CHUNK = 32
-EARLY = 16
-
-
-def east(q):
-    return pltpu.roll(q, LANES - 1, q.ndim - 1)
-
-
-def west(q):
-    return pltpu.roll(q, 1, q.ndim - 1)
+EARLY = 12
+BESIDE = 4
 
 
 def shifted(q, amount):
@@ -71,7 +64,6 @@
     Y,
     YT,
     DV,
-    HP,
     CLS,
     WHERE,
     VALUE,
@@ -163,9 +155,10 @@
         return carry
 
     lax.fori_loop(0, members + 2 * groups, clear, 0)
-    for padded in (Y.at[0], YT.at[0], YT.at[1], DV):
-        padded[0:PAD, :] = zero
-        padded[PAD + rows : PAD + rows + PAD, :] = zero
+    for k in range(BESIDE):
+        for padded in (Y.at[k], DV.at[k], YT.at[k, 0], YT.at[k, 1]):
+            padded[0:PAD, :] = zero
+            padded[PAD + rows : PAD + rows + PAD, :] = zero
 
     tall = (rows, 3 * rows)
     RT[...] = jnp.maximum(
@@ -182,7 +175,7 @@
         jnp.where((have % LANES) // radius == to // LANES, near, 0).astype(F32).astype(BF16)
     )
 
-    wide = (2 * LANES, LANES)
+    wide = (3 * LANES, LANES)
     ahead_by = (row_of(wide) - lane_of(wide)) % LANES
     DX[...] = (
         jnp.where(ahead_by == 1, HALF_DT, jnp.where(ahead_by == LANES - 1, -HALF_DT, 0.0))
@@ -201,31 +194,21 @@
     for i in range(1, FOLD):
         packed_depth = jnp.where(holder == i, shifted(depth, 8 + SPAN * i), packed_depth)
     QD[...] = packed_depth
-    SR[0] = shifted(packed_depth, -4)
-    SL[0] = shifted(packed_depth, -8)
-
     def pack_group(g, first, last):
-        def pack(f, carry):
+        for f in range(first, last):
             q = shifted(X[g * FOLD, f, inner, :], 8)
             for i in range(1, FOLD):
                 q = jnp.where(
                     holder == i, shifted(X[g * FOLD + i, f, inner, :], 8 + SPAN * i), q
                 )
             Q[g, f] = q
-            return carry
-
-        lax.fori_loop(first, last, pack, 0)
-
-    def edges(f, carry):
-        to_right = shifted(Q[0, f], -4)
-        to_left = shifted(Q[0, f], -8)
-        for g in range(1, groups):
-            mine = slot // 4 == g
-            to_right = jnp.where(mine, shifted(Q[g, f], 4 * g - 4), to_right)
-            to_left = jnp.where(mine, shifted(Q[g, f], 4 * g - 8), to_left)
-        SR[1 + f] = to_right
-        SL[1 + f] = to_left
-        return carry
+
+    def edges(f):
+        keep = (slot >= 4) & (slot < 12)
+        even = jnp.where(keep, Q[0, f], shifted(Q[1, f], 8))
+        odd = shifted(jnp.where(keep, Q[2, f], shifted(Q[3, f], 8)), 4)
+        SR[f] = jnp.where(slot % 8 >= 4, even, odd)
+        SL[f] = jnp.where(slot % 8 >= 4, odd, even)
 
     def send(source, target, there, send_sem, recv_sem):
         return pltpu.make_async_remote_copy(
@@ -237,30 +220,34 @@
             device_id_type=MESH,
         )
 
-    def edge_copies(tracers):
-        which = pl.ds(1 + flow, fields - flow) if tracers else pl.ds(0, 1 + flow)
-        k = int(tracers)
+    def edge_copies(f):
+        to_left, to_right = (QD, QD) if f == fields else (SL.at[f], SR.at[f])
         return (
-            send(SL.at[which], RR.at[which], left, edge_send.at[k, 0], edge_recv.at[k, 0]),
-            send(SR.at[which], RL.at[which], right, edge_send.at[k, 1], edge_recv.at[k, 1]),
-        )
+            send(to_left, RR.at[f], left, edge_send.at[f, 0], edge_recv.at[f, 0]),
+            send(to_right, RL.at[f], right, edge_send.at[f, 1], edge_recv.at[f, 1]),
+        )
+
+    travelling = [edge_copies(f) for f in range(fields + 1)]
+    moved_by = (0, -8, -4, -12)
+
+    def begin(f):
+        for copy in travelling[f]:
+            copy.start()
 
     for g in range(groups):
         load(g, False).wait()
-        pack_group(g, 0, flow)
-    lax.fori_loop(0, flow, edges, 0)
+        pack_group(g, 0, 1)
+    edges(0)
     pl.semaphore_wait(barrier, 2 + n_dom - 1)
-    flow_edges = edge_copies(False)
-    for copy in flow_edges:
-        copy.start()
-
-    for g in range(groups):
-        load(g, True).wait()
-        pack_group(g, flow, fields)
-    lax.fori_loop(flow, fields, edges, 0)
-    tracer_edges = edge_copies(True)
-    for copy in tracer_edges:
-        copy.start()
+    begin(fields)
+    begin(0)
+    for f in range(1, fields):
+        for g in range(groups):
+            if f == flow:
+                load(g, True).wait()
+            pack_group(g, f, f + 1)
+        edges(f)
+        begin(f)
 
     where = WHERE[...]
     value = VALUE[...]
@@ -295,90 +282,103 @@
     OBS[1] = mean_obs
     OBS[2] = -0.5 * (squares - total_obs * mean_obs)
 
-    def flow_step(h_ref, u_ref, v_ref, to_h, to_u, to_v, d):
-        for r in range(0, rows, CHUNK):
-            cut = pl.ds(r, CHUNK)
-            mid = pl.ds(PAD + r, CHUNK)
-            h = h_ref[mid, :]
-            u = u_ref(r)
-            v = v_ref(r)
-            u1 = u - HALF_DT * (east(h) - west(h)) + DT_F * v
-            slope = h_ref[pl.ds(PAD + r + 1, CHUNK), :] - h_ref[pl.ds(PAD + r - 1, CHUNK), :]
-            v1 = v - HALF_DT * slope - DT_F * u
-            to_u(r, u1)
-            to_v(r, v1)
-            deep = D[d, cut, :]
-            du = deep * u1
-            DV[mid, :] = deep * v1
-            HP[cut, :] = h - HALF_DT * (east(du) - west(du))
-        for r in range(0, rows, CHUNK):
-            up = DV[pl.ds(PAD + r + 1, CHUNK), :]
-            down = DV[pl.ds(PAD + r - 1, CHUNK), :]
-            to_h[pl.ds(PAD + r, CHUNK), :] = HP[pl.ds(r, CHUNK), :] - HALF_DT * (up - down)
-
-    def flow_ahead(m, d):
-        def get_x(f):
-            return lambda r: X[m, f, pl.ds(PAD + r, CHUNK), :]
-
-        def get_u(f):
-            return lambda r: U1[m, f, pl.ds(r, CHUNK), :]
-
-        def put_x(f):
-            def put(r, q):
-                X[m, f, pl.ds(PAD + r, CHUNK), :] = q
-
-            return put
-
-        def put_u(f):
-            def put(r, q):
-                U1[m, f, pl.ds(r, CHUNK), :] = q
-
-            return put
-
-        flow_step(X.at[m, 0], get_x(1), get_x(2), Y.at[0], put_u(0), put_u(1), d)
-        flow_step(Y.at[0], get_u(0), get_u(1), X.at[m, 0], put_x(1), put_x(2), d)
-
-    def tracers_ahead(m):
+    def split_in(q, count):
+        found = []
+        for k in range(count):
+            found.append(q.astype(BF16))
+            if k < count - 1:
+                q = q - found[-1].astype(F32)
+        return jnp.concatenate(found, axis=1)
+
+    def flow_ahead(ms, d):
         for step in range(2):
-            ends = [(X.at[m, f], YT.at[f - flow]) for f in range(flow, fields)]
+            ends = [(X.at[m, 0], Y.at[k]) for k, m in enumerate(ms)]
             if step == 1:
                 ends = [(target, source) for source, target in ends]
-            split = []
-            for source, _ in ends:
-                a = source[inner, :]
-                first = a.astype(BF16)
-                second = (a - first.astype(F32)).astype(BF16)
-                split.append(jnp.concatenate([first, second], axis=1))
-            across = dot(jnp.concatenate(split, axis=0), DX[...])
-            for r in range(0, rows, CHUNK):
-                mid = pl.ds(PAD + r, CHUNK)
-                if step == 0:
-                    u = U1[m, 0, pl.ds(r, CHUNK), :]
-                    v = U1[m, 1, pl.ds(r, CHUNK), :]
-                else:
-                    u = X[m, 1, mid, :]
-                    v = X[m, 2, mid, :]
-                v = HALF_DT * v
-                for k, (source, target) in enumerate(ends):
+            across = [dot(split_in(h_ref[inner, :], 3), DX[...]) for h_ref, _ in ends]
+            steep = []
+            for k, m in enumerate(ms):
+                h_ref = ends[k][0]
+                split = []
+                for r in range(0, rows, CHUNK):
+                    cut = pl.ds(r, CHUNK)
+                    mid = pl.ds(PAD + r, CHUNK)
+                    if step == 0:
+                        u, v = X[m, 1, mid, :], X[m, 2, mid, :]
+                    else:
+                        u, v = U1[m, 0, cut, :], U1[m, 1, cut, :]
+                    u1 = u - across[k][r : r + CHUNK, :] + DT_F * v
                     slope = (
-                        source[pl.ds(PAD + r + 1, CHUNK), :] - source[pl.ds(PAD + r - 1, CHUNK), :]
+                        h_ref[pl.ds(PAD + r + 1, CHUNK), :] - h_ref[pl.ds(PAD + r - 1, CHUNK), :]
                     )
-                    steep = across[k * rows + r : k * rows + r + CHUNK, :]
-                    target[mid, :] = source[mid, :] - (u * steep + v * slope)
+                    v1 = v - HALF_DT * slope - DT_F * u
+                    if step == 0:
+                        U1[m, 0, cut, :] = u1
+                        U1[m, 1, cut, :] = v1
+                    else:
+                        X[m, 1, mid, :] = u1
+                        X[m, 2, mid, :] = v1
+                    deep = D[d, cut, :]
+                    DV[k, mid, :] = deep * v1
+                    split.append(split_in(deep * u1, 3))
+                steep.append(dot(jnp.concatenate(split, axis=0), DX[...]))
+            for k, m in enumerate(ms):
+                h_ref, to_ref = ends[k]
+                for r in range(0, rows, CHUNK):
+                    mid = pl.ds(PAD + r, CHUNK)
+                    slope = DV[k, pl.ds(PAD + r + 1, CHUNK), :] - DV[k, pl.ds(PAD + r - 1, CHUNK), :]
+                    to_ref[mid, :] = h_ref[mid, :] - (
+                        steep[k][r : r + CHUNK, :] + HALF_DT * slope
+                    )
+
+    def tracers_ahead(ms):
+        for step in range(2):
+            steep = []
+            for k, m in enumerate(ms):
+                for f in range(flow, fields):
+                    source = X.at[m, f] if step == 0 else YT.at[k, f - flow]
+                    steep.append(split_in(source[inner, :], 2))
+            steep = [
+                dot(jnp.concatenate(steep[2 * k : 2 * k + 2], axis=0), DX[0 : 2 * LANES, :])
+                for k in range(len(ms))
+            ]
+            for k, m in enumerate(ms):
+                ends = [(X.at[m, f], YT.at[k, f - flow]) for f in range(flow, fields)]
+                if step == 1:
+                    ends = [(target, source) for source, target in ends]
+                for r in range(0, rows, CHUNK):
+                    mid = pl.ds(PAD + r, CHUNK)
+                    if step == 0:
+                        u = U1[m, 0, pl.ds(r, CHUNK), :]
+                        v = U1[m, 1, pl.ds(r, CHUNK), :]
+                    else:
+                        u = X[m, 1, mid, :]
+                        v = X[m, 2, mid, :]
+                    v = HALF_DT * v
+                    for j, (source, target) in enumerate(ends):
+                        slope = (
+                            source[pl.ds(PAD + r + 1, CHUNK), :]
+                            - source[pl.ds(PAD + r - 1, CHUNK), :]
+                        )
+                        across = steep[k][j * rows + r : j * rows + r + CHUNK, :]
+                        target[mid, :] = source[mid, :] - (u * across + v * slope)
+
+    def some(first):
+        return [first + k for k in range(BESIDE)]
 
     def flow_main(m, carry):
-        flow_ahead(m, 0)
+        flow_ahead(some(BESIDE * m), 0)
         return carry
 
     early = EARLY
-    lax.fori_loop(0, early, flow_main, 0)
+    lax.fori_loop(0, early // BESIDE, flow_main, 0)
 
     def strips(f, carry):
         for g in range(groups):
             q = Q[g, f]
-            X[members + g, f, inner, :] = jnp.where(slot < 8, q, shifted(RR[1 + f], 8 - 4 * g))
+            X[members + g, f, inner, :] = jnp.where(slot < 8, q, shifted(RR[f], moved_by[g]))
             X[members + groups + g, f, inner, :] = jnp.where(
-                slot >= 8, q, shifted(RL[1 + f], 4 - 4 * g)
+                slot >= 8, q, shifted(RL[f], moved_by[g])
             )
         return carry
 
@@ -389,17 +389,18 @@
             )
         return carry
 
-    for copy in flow_edges:
-        copy.wait()
-    D[1] = jnp.where(slot < 8, QD[...], shifted(RR[0], 8))
-    D[2] = jnp.where(slot >= 8, QD[...], shifted(RL[0], 4))
+    for f in (fields, 0, 1, 2):
+        for copy in travelling[f]:
+            copy.wait()
+    D[1] = jnp.where(slot < 8, QD[...], RR[fields])
+    D[2] = jnp.where(slot >= 8, QD[...], RL[fields])
     lax.fori_loop(0, flow, strips, 0)
 
     def flow_strip(s, carry):
-        flow_ahead(members + s, 1 + s // groups)
-        return carry
-
-    lax.fori_loop(0, 2 * groups, flow_strip, 0)
+        flow_ahead(some(members + BESIDE * s), 1 + BESIDE * s // groups)
+        return carry
+
+    lax.fori_loop(0, 2 * groups // BESIDE, flow_strip, 0)
     join(0, 0)
 
     at_edge = (lane < 4) | (lane >= LANES - 4)
@@ -413,43 +414,50 @@
     def halo_right(p):
         return send(TOR.at[p], HL.at[p], right, halo_send.at[1, p], halo_recv.at[1, p])
 
-    def likelihood(p, carry):
-        both = []
-        for k in range(2):
-            m = 2 * p + k
-            edge = pltpu.roll(FE[m // FOLD, 0], place(lax.rem(m, FOLD)), 1)
-            h = jnp.where(at_edge, edge, X[m, 0, inner, :])
-            miss = OBS[1] - h
-            both.append(OBS[0] * (miss * miss) + OBS[2])
-        a, b, c = pieces(jnp.concatenate(both, axis=1))
-        smooth = dot(RT[...], jnp.concatenate([a, b, c], axis=0))
-        SM[p] = smooth
-        first, second = smooth[:, :LANES], smooth[:, LANES:]
-        low = lane < radius
-        turned = shifted(jnp.where(low, second, first), radius)
-        TOL[p] = jnp.where(low, first, turned)
-        TOR[p] = jnp.where(low, turned, second)
-        halo_left(p).start()
-        halo_right(p).start()
-        return carry
-
-    def flow_and_likelihood(p, carry):
-        ahead = p + early // 2
-        flow_ahead(2 * ahead, 0)
-        flow_ahead(2 * ahead + 1, 0)
-        return likelihood(p, carry)
-
-    lax.fori_loop(0, pairs - early // 2, flow_and_likelihood, 0)
-    lax.fori_loop(pairs - early // 2, pairs, likelihood, 0)
+    def likelihood(ps):
+        logs = []
+        for p in ps:
+            both = []
+            for k in range(2):
+                m = 2 * p + k
+                edge = pltpu.roll(FE[m // FOLD, 0], place(lax.rem(m, FOLD)), 1)
+                h = jnp.where(at_edge, edge, X[m, 0, inner, :])
+                miss = OBS[1] - h
+                both.append(OBS[0] * (miss * miss) + OBS[2])
+            logs.append(jnp.concatenate(both, axis=1))
+        smoothed = [dot(RT[...], jnp.concatenate(pieces(q), axis=0)) for q in logs]
+        for p, smooth in zip(ps, smoothed):
+            SM[p] = smooth
+            first, second = smooth[:, :LANES], smooth[:, LANES:]
+            low = lane < radius
+            turned = shifted(jnp.where(low, second, first), radius)
+            TOL[p] = jnp.where(low, first, turned)
+            TOR[p] = jnp.where(low, turned, second)
+            halo_left(p).start()
+            halo_right(p).start()
+
+    def flow_and_likelihood(q, carry):
+        flow_ahead(some(BESIDE * q + early), 0)
+        likelihood([2 * q, 2 * q + 1])
+        return carry
+
+    def only_likelihood(q, carry):
+        likelihood([2 * q, 2 * q + 1])
+        return carry
+
+    both_ways = (members - early) // BESIDE
+    lax.fori_loop(0, both_ways, flow_and_likelihood, 0)
+    lax.fori_loop(both_ways, pairs // 2, only_likelihood, 0)
 
     def tracers_main(m, carry):
-        tracers_ahead(m)
-        return carry
-
-    for copy in tracer_edges:
-        copy.wait()
+        tracers_ahead(some(BESIDE * m))
+        return carry
+
+    for f in range(flow, fields):
+        for copy in travelling[f]:
+            copy.wait()
     lax.fori_loop(flow, fields, strips, 0)
-    lax.fori_loop(0, members + 2 * groups, tracers_main, 0, unroll=4)
+    lax.fori_loop(0, (members + 2 * groups) // BESIDE, tracers_main, 0)
     lax.fori_loop(1, fields, join, 0)
 
     def columns(q, table):
@@ -590,10 +598,9 @@
             scratch_shapes=[
                 pltpu.VMEM((members + 2 * groups, fields, tall, lanes), F32),
                 pltpu.VMEM((members + 2 * groups, 2, rows, lanes), F32),
-                pltpu.VMEM((1, tall, lanes), F32),
-                pltpu.VMEM((2, tall, lanes), F32),
-                pltpu.VMEM((tall, lanes), F32),
-                pltpu.VMEM((rows, lanes), F32),
+                pltpu.VMEM((BESIDE, tall, lanes), F32),
+                pltpu.VMEM((BESIDE, 2, tall, lanes), F32),
+                pltpu.VMEM((BESIDE, tall, lanes), F32),
                 pltpu.VMEM((rows, lanes), jnp.int32),
                 pltpu.VMEM((obs_index.shape[0] // lanes, lanes), jnp.int32),
                 pltpu.VMEM((obs_index.shape[0] // lanes, lanes), F32),
@@ -602,8 +609,8 @@
                 pltpu.VMEM((rows, lanes), F32),
                 pltpu.VMEM((groups, fields, rows, lanes), F32),
                 pltpu.VMEM((groups, fields, rows, lanes), F32),
-                pltpu.VMEM((fields + 1, rows, lanes), F32),
-                pltpu.VMEM((fields + 1, rows, lanes), F32),
+                pltpu.VMEM((fields, rows, lanes), F32),
+                pltpu.VMEM((fields, rows, lanes), F32),
                 pltpu.VMEM((fields + 1, rows, lanes), F32),
                 pltpu.VMEM((fields + 1, rows, lanes), F32),
                 pltpu.VMEM((3, rows, lanes), F32),
@@ -619,11 +626,11 @@
                 pltpu.VMEM((rows, 3 * rows), BF16),
                 pltpu.VMEM((2 * lanes, 2 * lanes), BF16),
                 pltpu.VMEM((2 * lanes, 2 * lanes), BF16),
-                pltpu.VMEM((2 * lanes, lanes), BF16),
+                pltpu.VMEM((3 * lanes, lanes), BF16),
                 dma((4,)),
                 dma((2, groups)),
-                dma((2, 2)),
-                dma((2, 2)),
+                dma((fields + 1, 2)),
+                dma((fields + 1, 2)),
                 dma((2, pairs)),
                 dma((2, pairs)),
                 dma((n_dom - 1,)),

time: 46.6 us -> 42.4 us (0.910)
  Pallas kernels: 44.8 us -> 40.6 us
    pallas_call x1, Pallas kernels: 44.8 us -> 40.6 us  [on_device(): pl.pallas_call(functools.partial(kernel, n_dom, n_col), out_shape=jax.Sha...]
where the time goes in v2:
time: 42.4 us; the launch traced here: 42.2 us
  Pallas kernels  40.6 us (96%)
  local copies, waits for them, and re-layouts  1.65 us (4%)
    pallas_call x1, Pallas kernels, on_device(): pl.pallas_call(functools.partial(kernel, n_dom, n_col), out_shape=jax.Sha...  40.6 us
    unnamed x1, local copies, waits for them, and re-layouts  1.65 us

profile of v2, /device:TPU:0, one launch (start us, length us, event | category | flops | bytes accessed | tf_op | source)
XLA Modules:
  0.0 42.2 jit_solution(579204428516042280)
XLA Ops:
  0.0 40.6 %shard_map.55 = f32[5,96,128]{2,1,0:T(8,128)} custom-call(f32[32,5,96,128]{3,2,1,0:T(8,128)} %ens_ref.1, s32[96,128]{1,0:T(8,128)} %class_ref.1, s32[6,128]{1,0:T(8,128)} %bitcast.2, f32[6,128]{1,0:T(8,128)} %bitcast.3, f32[96,128]{1,0:T(8,128)} %anneal_ref.1), custom_call_target="tpu_custom_call" | custom-call | flops 200000000 | bytes 9000000 | tf_op jit(solution)/shard_map/pallas_call | solution.py:593
  40.6 1.7 %copy.7 = f32[5,96,128]{2,1,0:T(8,128)} copy(f32[5,96,128]{2,1,0:T(8,128)} %shard_map.55) | data formatting | bytes 491520

commit v3 on v2

--- a/solution.py
+++ b/solution.py
@@ -24,6 +24,7 @@
 CHUNK = 32
 EARLY = 12
 BESIDE = 4
+HALF_BAND = 16
 
 
 def shifted(q, amount):
@@ -86,6 +87,8 @@
     LW,
     GIVE,
     TAKE,
+    DONE,
+    FETCHED,
     RT,
     WOWN,
     WHALO,
@@ -104,7 +107,8 @@
     members, fields, rows, _ = ens_ref.shape
     groups = members // FOLD
     pairs = members // 2
-    share = rows // n_dom
+    share = 8
+    band = share * n_dom
     radius = LANES // 2
     flow = 3
     me_dom = lax.axis_index("dom")
@@ -408,11 +412,25 @@
     def place(i):
         return lax.rem(LANES + LANES - 8 - SPAN * i, LANES)
 
-    def halo_left(p):
-        return send(TOL.at[p], HR.at[p], left, halo_send.at[0, p], halo_recv.at[0, p])
-
-    def halo_right(p):
-        return send(TOR.at[p], HL.at[p], right, halo_send.at[1, p], halo_recv.at[1, p])
+    upper = rows - band
+
+    def halo_pair(p):
+        here = pl.ds(0, upper)
+        return (
+            send(TOL.at[p, here], HR.at[p, here], left, halo_send.at[0, p], halo_recv.at[0, p]),
+            send(TOR.at[p, here], HL.at[p, here], right, halo_send.at[1, p], halo_recv.at[1, p]),
+        )
+
+    def halo_rest():
+        here = pl.ds(upper, band)
+        return (
+            send(
+                TOL.at[:, here], HR.at[:, here], left, halo_send.at[0, pairs], halo_recv.at[0, pairs]
+            ),
+            send(
+                TOR.at[:, here], HL.at[:, here], right, halo_send.at[1, pairs], halo_recv.at[1, pairs]
+            ),
+        )
 
     def likelihood(ps):
         logs = []
@@ -433,8 +451,8 @@
             turned = shifted(jnp.where(low, second, first), radius)
             TOL[p] = jnp.where(low, first, turned)
             TOR[p] = jnp.where(low, turned, second)
-            halo_left(p).start()
-            halo_right(p).start()
+            for copy in halo_pair(p):
+                copy.start()
 
     def flow_and_likelihood(q, carry):
         flow_ahead(some(BESIDE * q + early), 0)
@@ -448,6 +466,8 @@
     both_ways = (members - early) // BESIDE
     lax.fori_loop(0, both_ways, flow_and_likelihood, 0)
     lax.fori_loop(both_ways, pairs // 2, only_likelihood, 0)
+    for copy in halo_rest():
+        copy.start()
 
     def tracers_main(m, carry):
         tracers_ahead(some(BESIDE * m))
@@ -471,27 +491,23 @@
     lax.fori_loop(0, pairs, own_columns, 0, unroll=4)
 
     def halo_wait(p, carry):
-        halo_left(p).wait()
-        halo_right(p).wait()
-        return carry
-
-    lax.fori_loop(0, pairs, halo_wait, 0)
+        for copy in halo_pair(p):
+            copy.wait()
+        return carry
 
     scale = 1.0 / ((ROW_REACH + 1.0) * (radius + 1.0))
-    cut = (share, LANES)
+    cut = (HALF_BAND, LANES)
     cut_lane = lane_of(cut)
     cut_edge = (cut_lane < 4) | (cut_lane >= LANES - 4)
-    cut_holder = (cut_lane) // SPAN
-
-    def weigh(b, slot_out):
-        start = pl.multiple_of(b * share, 8)
-        here = pl.ds(start, share)
-        there = pl.ds(PAD + start, share)
+    cut_holder = cut_lane // SPAN
+
+    def weigh(b):
+        here = pl.ds(b * band, band)
         halo = jnp.concatenate([HR[:, here, :], HL[:, here, :]], axis=2)
-        smooth = PART[:, here, :].reshape(pairs * share, 2 * LANES) + columns(
-            halo.reshape(pairs * share, 2 * LANES), WHALO[...]
-        )
-        smooth = smooth.reshape(pairs, share, 2 * LANES)
+        smooth = PART[:, here, :].reshape(pairs * band, 2 * LANES) + columns(
+            halo.reshape(pairs * band, 2 * LANES), WHALO[...]
+        )
+        smooth = smooth.reshape(pairs, band, 2 * LANES)
         power = ANNEAL[here, :] * scale
         peak = None
         for p in range(pairs):
@@ -499,83 +515,102 @@
                 logw = power * smooth[p, :, k * LANES : (k + 1) * LANES]
                 LW[2 * p + k] = logw
                 peak = logw if peak is None else jnp.maximum(peak, logw)
-        total = jnp.zeros(cut, F32)
-        sums = [jnp.zeros(cut, F32) for _ in range(fields)]
-        edge_sums = [jnp.zeros(cut, F32) for _ in range(fields)]
-        for g in range(groups):
-            packed = None
-            for i in range(FOLD):
-                m = g * FOLD + i
-                w = jnp.exp(LW[m] - peak)
-                total = total + w
+        def set_out(f, start, q):
+            for d in range(start // share, (start + q.shape[0]) // share):
+                GIVE[b, d, f] = q[d * share - start : (d + 1) * share - start, :]
+
+        set_out(0, 0, peak)
+        for start in range(0, band, HALF_BAND):
+            within = pl.ds(start, HALF_BAND)
+            here = pl.ds(b * band + start, HALF_BAND)
+            there = pl.ds(PAD + b * band + start, HALF_BAND)
+            best = peak[start : start + HALF_BAND, :]
+            total = jnp.zeros(cut, F32)
+            sums = [jnp.zeros(cut, F32) for _ in range(fields)]
+            edge_sums = [jnp.zeros(cut, F32) for _ in range(fields)]
+            for g in range(groups):
+                packed = None
+                for i in range(FOLD):
+                    m = g * FOLD + i
+                    w = jnp.exp(LW[m, within, :] - best)
+                    total = total + w
+                    for f in range(fields):
+                        sums[f] = sums[f] + w * X[m, f, there, :]
+                    moved = shifted(w, 8 + SPAN * i)
+                    packed = moved if packed is None else jnp.where(cut_holder == i, moved, packed)
                 for f in range(fields):
-                    sums[f] = sums[f] + w * X[m, f, there, :]
-                moved = shifted(w, 8 + SPAN * i)
-                packed = moved if packed is None else jnp.where(cut_holder == i, moved, packed)
+                    edge_sums[f] = edge_sums[f] + packed * FE[g, f, here, :]
+            set_out(1, start, total)
             for f in range(fields):
-                edge_sums[f] = edge_sums[f] + packed * FE[g, f, here, :]
-        GIVE[slot_out, 0] = peak
-        GIVE[slot_out, 1] = total
-        for f in range(fields):
-            e = edge_sums[f]
-            e = e + shifted(e, SPAN)
-            e = e + shifted(e, 2 * SPAN)
-            e = e + shifted(e, 4 * SPAN)
-            GIVE[slot_out, 2 + f] = jnp.where(cut_edge, shifted(e, LANES - 8), sums[f])
-
-    def give(off):
+                e = edge_sums[f]
+                e = e + shifted(e, SPAN)
+                e = e + shifted(e, 2 * SPAN)
+                e = e + shifted(e, 4 * SPAN)
+                set_out(2 + f, start, jnp.where(cut_edge, shifted(e, LANES - 8), sums[f]))
+
+    def give(b, off):
+        owner = lax.rem(me_dom + off, n_dom)
         return pltpu.make_async_remote_copy(
-            src_ref=GIVE.at[off],
-            dst_ref=TAKE.at[off - 1],
-            send_sem=part_send.at[off - 1],
-            recv_sem=part_recv.at[off - 1],
+            src_ref=GIVE.at[b, owner],
+            dst_ref=TAKE.at[b, off - 1],
+            send_sem=part_send.at[b, off - 1],
+            recv_sem=part_recv.at[b, off - 1],
+            device_id=(owner, me_col),
+            device_id_type=MESH,
+        )
+
+    def hand_out(b, off):
+        return pltpu.make_async_remote_copy(
+            src_ref=DONE.at[b],
+            dst_ref=FETCHED.at[b, off - 1],
+            send_sem=out_send.at[b, off - 1],
+            recv_sem=out_recv.at[b, off - 1],
             device_id=(lax.rem(me_dom + off, n_dom), me_col),
             device_id_type=MESH,
         )
 
-    def offset(j):
-        return 2 + j - 3 * (j // 2)
-
-    def weigh_others(j, carry):
-        off = offset(j)
-        weigh(lax.rem(me_dom + off, n_dom), off)
-        give(off).start()
-        return carry
-
-    lax.fori_loop(0, n_dom - 1, weigh_others, 0)
-    weigh(me_dom, 0)
-    for off in range(1, n_dom):
-        give(off).wait()
-
-    peaks = [GIVE[0, 0]] + [TAKE[k, 0] for k in range(n_dom - 1)]
-    peak = functools.reduce(jnp.maximum, peaks)
-    factors = [jnp.exp(q - peak) for q in peaks]
-
-    def joined(f):
-        result = factors[0] * GIVE[0, f]
-        for k in range(n_dom - 1):
-            result = result + factors[k + 1] * TAKE[k, f]
-        return result
-
-    total = joined(1)
-    here = pl.ds(pl.multiple_of(me_dom * share, 8), share)
-    for f in range(fields):
-        out_ref[f, here, :] = joined(2 + f) / total
-
-    def hand_out(off):
-        return pltpu.make_async_remote_copy(
-            src_ref=out_ref.at[:, here, :],
-            dst_ref=out_ref.at[:, here, :],
-            send_sem=out_send.at[off - 1],
-            recv_sem=out_recv.at[off - 1],
-            device_id=(lax.rem(me_dom + off, n_dom), me_col),
-            device_id_type=MESH,
-        )
-
-    for off in range(1, n_dom):
-        hand_out(off).start()
-    for off in range(1, n_dom):
-        hand_out(off).wait()
+    far_first = (2, 1, 3)
+
+    def join_band(b):
+        for off in far_first:
+            give(b, off).wait()
+        peaks = [GIVE[b, me_dom, 0]] + [TAKE[b, k, 0] for k in range(n_dom - 1)]
+        peak = functools.reduce(jnp.maximum, peaks)
+        factors = [jnp.exp(q - peak) for q in peaks]
+
+        def joined(f):
+            result = factors[0] * GIVE[b, me_dom, f]
+            for k in range(n_dom - 1):
+                result = result + factors[k + 1] * TAKE[b, k, f]
+            return result
+
+        total = joined(1)
+        for f in range(fields):
+            DONE[b, f] = joined(2 + f) / total
+        for off in far_first:
+            hand_out(b, off).start()
+
+    bands = rows // band
+    lax.fori_loop(0, pairs, halo_wait, 0)
+    for b in range(bands):
+        if b == bands - 1:
+            for copy in halo_rest():
+                copy.wait()
+        weigh(b)
+        for off in far_first:
+            give(b, off).start()
+    for b in range(bands):
+        join_band(b)
+    def place_rows(b, d, source):
+        here = pl.ds(pl.multiple_of(b * band + d * share, 8), share)
+        for f in range(fields):
+            out_ref[f, here, :] = source[f]
+
+    for b in range(bands):
+        place_rows(b, me_dom, DONE.at[b])
+        for off in far_first:
+            hand_out(b, off).wait()
+            place_rows(b, lax.rem(me_dom + n_dom - off, n_dom), FETCHED.at[b, off - 1])
 
 
 def solution(mesh):
@@ -586,7 +621,9 @@
         members, fields, rows, lanes = ensemble.shape
         groups = members // FOLD
         pairs = members // 2
-        share = rows // n_dom
+        share = 8
+        band = share * n_dom
+        bands = rows // band
         tall = rows + 2 * PAD
         vm = pl.BlockSpec(memory_space=pltpu.VMEM)
         dma = pltpu.SemaphoreType.DMA
@@ -620,9 +657,11 @@
                 pltpu.VMEM((pairs, rows, lanes), F32),
                 pltpu.VMEM((pairs, rows, lanes), F32),
                 pltpu.VMEM((pairs, rows, lanes), F32),
-                pltpu.VMEM((members, share, lanes), F32),
-                pltpu.VMEM((n_dom, fields + 2, share, lanes), F32),
-                pltpu.VMEM((n_dom - 1, fields + 2, share, lanes), F32),
+                pltpu.VMEM((members, band, lanes), F32),
+                pltpu.VMEM((bands, n_dom, fields + 2, share, lanes), F32),
+                pltpu.VMEM((bands, n_dom - 1, fields + 2, share, lanes), F32),
+                pltpu.VMEM((bands, fields, share, lanes), F32),
+                pltpu.VMEM((bands, n_dom - 1, fields, share, lanes), F32),
                 pltpu.VMEM((rows, 3 * rows), BF16),
                 pltpu.VMEM((2 * lanes, 2 * lanes), BF16),
                 pltpu.VMEM((2 * lanes, 2 * lanes), BF16),
@@ -631,12 +670,12 @@
                 dma((2, groups)),
                 dma((fields + 1, 2)),
                 dma((fields + 1, 2)),
-                dma((2, pairs)),
-                dma((2, pairs)),
-                dma((n_dom - 1,)),
-                dma((n_dom - 1,)),
-                dma((n_dom - 1,)),
-                dma((n_dom - 1,)),
+                dma((2, pairs + 1)),
+                dma((2, pairs + 1)),
+                dma((bands, n_dom - 1)),
+                dma((bands, n_dom - 1)),
+                dma((bands, n_dom - 1)),
+                dma((bands, n_dom - 1)),
             ],
             compiler_params=pltpu.CompilerParams(
                 collective_id=0, has_side_effects=True, vmem_limit_bytes=62 * 1024 * 1024

time: 42.4 us -> 40.8 us (0.962)
  Pallas kernels: 40.6 us -> 39 us
    pallas_call x1, Pallas kernels: 40.6 us -> 39 us  [on_device(): pl.pallas_call(functools.partial(kernel, n_dom, n_col), out_shape=jax.Sha...]
where the time goes in v3:
time: 40.8 us; the launch traced here: 40.6 us
  Pallas kernels  39 us (96%)
  local copies, waits for them, and re-layouts  1.65 us (4%)
    pallas_call x1, Pallas kernels, on_device(): pl.pallas_call(functools.partial(kernel, n_dom, n_col), out_shape=jax.Sha...  39 us
    unnamed x1, local copies, waits for them, and re-layouts  1.65 us

profile of v3, /device:TPU:0, one launch (start us, length us, event | category | flops | bytes accessed | tf_op | source)
XLA Modules:
  0.0 40.6 jit_solution(2033675319442685482)
XLA Ops:
  0.0 39.0 %shard_map.55 = f32[5,96,128]{2,1,0:T(8,128)} custom-call(f32[32,5,96,128]{3,2,1,0:T(8,128)} %ens_ref.1, s32[96,128]{1,0:T(8,128)} %class_ref.1, s32[6,128]{1,0:T(8,128)} %bitcast.2, f32[6,128]{1,0:T(8,128)} %bitcast.3, f32[96,128]{1,0:T(8,128)} %anneal_ref.1), custom_call_target="tpu_custom_call" | custom-call | flops 200000000 | bytes 9000000 | tf_op jit(solution)/shard_map/pallas_call | solution.py:630
  39.0 1.7 %copy.7 = f32[5,96,128]{2,1,0:T(8,128)} copy(f32[5,96,128]{2,1,0:T(8,128)} %shard_map.55) | data formatting | bytes 491520

commit v4 on v3

--- a/solution.py
+++ b/solution.py
@@ -22,7 +22,7 @@
 FOLD = 8
 SPAN = 16
 CHUNK = 32
-EARLY = 12
+EARLY = 16
 BESIDE = 4
 HALF_BAND = 16
 
@@ -164,27 +164,6 @@
             padded[0:PAD, :] = zero
             padded[PAD + rows : PAD + rows + PAD, :] = zero
 
-    tall = (rows, 3 * rows)
-    RT[...] = jnp.maximum(
-        0, ROW_REACH + 1 - jnp.abs(row_of(tall) - lane_of(tall) % rows)
-    ).astype(F32).astype(BF16)
-    wide = (2 * LANES, 2 * LANES)
-    to = lane_of(wide)
-    have = row_of(wide)
-    near = jnp.maximum(0, radius + 1 - jnp.abs(have % LANES - to % LANES))
-    WOWN[...] = jnp.where(have // LANES == to // LANES, near, 0).astype(F32).astype(BF16)
-    column = have % radius + jnp.where(have < LANES, LANES, -radius)
-    near = jnp.maximum(0, radius + 1 - jnp.abs(column - to % LANES))
-    WHALO[...] = (
-        jnp.where((have % LANES) // radius == to // LANES, near, 0).astype(F32).astype(BF16)
-    )
-
-    wide = (3 * LANES, LANES)
-    ahead_by = (row_of(wide) - lane_of(wide)) % LANES
-    DX[...] = (
-        jnp.where(ahead_by == 1, HALF_DT, jnp.where(ahead_by == LANES - 1, -HALF_DT, 0.0))
-    ).astype(BF16)
-
     for copy in small:
         copy.wait()
 
@@ -252,6 +231,27 @@
             pack_group(g, f, f + 1)
         edges(f)
         begin(f)
+
+    tall = (rows, 3 * rows)
+    RT[...] = jnp.maximum(
+        0, ROW_REACH + 1 - jnp.abs(row_of(tall) - lane_of(tall) % rows)
+    ).astype(F32).astype(BF16)
+    wide = (2 * LANES, 2 * LANES)
+    to = lane_of(wide)
+    have = row_of(wide)
+    near = jnp.maximum(0, radius + 1 - jnp.abs(have % LANES - to % LANES))
+    WOWN[...] = jnp.where(have // LANES == to // LANES, near, 0).astype(F32).astype(BF16)
+    column = have % radius + jnp.where(have < LANES, LANES, -radius)
+    near = jnp.maximum(0, radius + 1 - jnp.abs(column - to % LANES))
+    WHALO[...] = (
+        jnp.where((have % LANES) // radius == to // LANES, near, 0).astype(F32).astype(BF16)
+    )
+
+    wide = (3 * LANES, LANES)
+    ahead_by = (row_of(wide) - lane_of(wide)) % LANES
+    DX[...] = (
+        jnp.where(ahead_by == 1, HALF_DT, jnp.where(ahead_by == LANES - 1, -HALF_DT, 0.0))
+    ).astype(BF16)
 
     where = WHERE[...]
     value = VALUE[...]
@@ -456,7 +456,7 @@
 
     def flow_and_likelihood(q, carry):
         flow_ahead(some(BESIDE * q + early), 0)
-        likelihood([2 * q, 2 * q + 1])
+        likelihood([2 * q + 2, 2 * q + 3])
         return carry
 
     def only_likelihood(q, carry):
@@ -464,8 +464,9 @@
         return carry
 
     both_ways = (members - early) // BESIDE
+    likelihood([0, 1])
     lax.fori_loop(0, both_ways, flow_and_likelihood, 0)
-    lax.fori_loop(both_ways, pairs // 2, only_likelihood, 0)
+    lax.fori_loop(both_ways + 1, pairs // 2, only_likelihood, 0)
     for copy in halo_rest():
         copy.start()
 

time: 40.8 us -> 40.3 us (0.988)
  Pallas kernels: 39 us -> 38.5 us
    pallas_call x1, Pallas kernels: 39 us -> 38.5 us  [on_device(): pl.pallas_call(functools.partial(kernel, n_dom, n_col), out_shape=jax.Sha...]
where the time goes in v4:
time: 40.3 us; the launch traced here: 40.2 us
  Pallas kernels  38.5 us (96%)
  local copies, waits for them, and re-layouts  1.65 us (4%)
    pallas_call x1, Pallas kernels, on_device(): pl.pallas_call(functools.partial(kernel, n_dom, n_col), out_shape=jax.Sha...  38.5 us
    unnamed x1, local copies, waits for them, and re-layouts  1.65 us

profile of v4, /device:TPU:0, one launch (start us, length us, event | category | flops | bytes accessed | tf_op | source)
XLA Modules:
  0.0 40.2 jit_solution(6002112594499072501)
XLA Ops:
  0.0 38.5 %shard_map.55 = f32[5,96,128]{2,1,0:T(8,128)} custom-call(f32[32,5,96,128]{3,2,1,0:T(8,128)} %ens_ref.1, s32[96,128]{1,0:T(8,128)} %class_ref.1, s32[6,128]{1,0:T(8,128)} %bitcast.2, f32[6,128]{1,0:T(8,128)} %bitcast.3, f32[96,128]{1,0:T(8,128)} %anneal_ref.1), custom_call_target="tpu_custom_call" | custom-call | flops 200000000 | bytes 9000000 | tf_op jit(solution)/shard_map/pallas_call | solution.py:631
  38.5 1.7 %copy.7 = f32[5,96,128]{2,1,0:T(8,128)} copy(f32[5,96,128]{2,1,0:T(8,128)} %shard_map.55) | data formatting | bytes 491520

commit v5 on v4

--- a/solution.py
+++ b/solution.py
@@ -22,7 +22,7 @@
 FOLD = 8
 SPAN = 16
 CHUNK = 32
-EARLY = 16
+EARLY = 20
 BESIDE = 4
 HALF_BAND = 16
 
@@ -489,7 +489,7 @@
         PART[p] = columns(SM[p], WOWN[...])
         return carry
 
-    lax.fori_loop(0, pairs, own_columns, 0, unroll=4)
+    lax.fori_loop(0, pairs, own_columns, 0, unroll=8)
 
     def halo_wait(p, carry):
         for copy in halo_pair(p):

time: 40.3 us -> 40.8 us (1.012)
  Pallas kernels: 38.5 us -> 39 us
    pallas_call x1, Pallas kernels: 38.5 us -> 39 us  [on_device(): pl.pallas_call(functools.partial(kernel, n_dom, n_col), out_shape=jax.Sha...]
where the time goes in v5:
time: 40.8 us; the launch traced here: 40.7 us
  Pallas kernels  39 us (96%)
  local copies, waits for them, and re-layouts  1.65 us (4%)
    pallas_call x1, Pallas kernels, on_device(): pl.pallas_call(functools.partial(kernel, n_dom, n_col), out_shape=jax.Sha...  39 us
    unnamed x1, local copies, waits for them, and re-layouts  1.65 us

profile of v5, /device:TPU:0, one launch (start us, length us, event | category | flops | bytes accessed | tf_op | source)
XLA Modules:
  0.0 40.7 jit_solution(14525792602662655225)
XLA Ops:
  0.0 39.0 %shard_map.55 = f32[5,96,128]{2,1,0:T(8,128)} custom-call(f32[32,5,96,128]{3,2,1,0:T(8,128)} %ens_ref.1, s32[96,128]{1,0:T(8,128)} %class_ref.1, s32[6,128]{1,0:T(8,128)} %bitcast.2, f32[6,128]{1,0:T(8,128)} %bitcast.3, f32[96,128]{1,0:T(8,128)} %anneal_ref.1), custom_call_target="tpu_custom_call" | custom-call | flops 200000000 | bytes 9000000 | tf_op jit(solution)/shard_map/pallas_call | solution.py:631
  39.0 1.7 %copy.7 = f32[5,96,128]{2,1,0:T(8,128)} copy(f32[5,96,128]{2,1,0:T(8,128)} %shard_map.55) | data formatting | bytes 491520
